TPU v7x, 32 devices: a whole 2x2x4 slice. The times are simulated.
32 devices in a mesh: ctx: 4 (over x, core), tp: 8 (over z, y).
Axes of the slice: x: 2, y: 2, z: 4, core: 2. Of those that a mesh axis runs over, the one named last changes fastest.
Arguments:
- lin_query: bfloat16 [2048, 8, 128], P('ctx', 'tp'), may hold values from -6 to 6
- lin_key: bfloat16 [2048, 8, 128], P('ctx', 'tp'), may hold values from -6 to 6
- lin_value: bfloat16 [2048, 8, 128], P('ctx', 'tp'), may hold values from -6 to 6
- log_decay: float32 [8, 2048], P('tp', 'ctx'), may hold values from -2 to 0, as said below
- soft_query: bfloat16 [2048, 8, 128], P('ctx', 'tp'), may hold values from -12 to 12
- soft_key: bfloat16 [2048, 8, 128], P('ctx', 'tp'), may hold values from -4 to 4
- soft_value: bfloat16 [2048, 8, 128], P('ctx', 'tp'), may hold values from -6 to 6
Outputs:
- linear_out: bfloat16 [2048, 8, 128], P('ctx', 'tp')
- softmax_out: bfloat16 [2048, 8, 128], P('ctx', 'tp')
Inputs may be any that keep to these rules, and one draw needn't show every extreme that they name: `log_decay`: every entry is negative.
All inputs are finite; a program needn't handle non-finite values.
Results may differ from a plain program's by a relative error of at most 0.0055.
Values may be sent and summed in bfloat16 or wider, within the bound.
No kernel may reach another device: no remote copies, remote signals or barrier semaphores. Data moves between devices by JAX's collectives and lax.ppermute only.
A program may use at most 64 MiB of HBM per device.

v0:
```python
import math

import jax
import jax.numpy as jnp
from jax import lax
from jax.sharding import PartitionSpec as P


def lightning_block(lin_query, lin_key, lin_value, log_decay):
    rows = lin_query.shape[0]
    heads = lin_query.shape[1]
    cum = jnp.cumsum(log_decay, axis=1)
    lower = jnp.arange(rows)[:, None] >= jnp.arange(rows)[None, :]
    diff = cum[:, :, None] - cum[:, None, :]
    mask = jnp.exp(jnp.where(lower[None], diff, -1e30))
    scores = jnp.einsum("thd,shd->hts", lin_query, lin_key, preferred_element_type=jnp.float32)
    weights = (scores * mask).astype(jnp.bfloat16)
    intra = jnp.einsum("hts,she->the", weights, lin_value, preferred_element_type=jnp.float32)
    last = cum[:, -1]
    decayed = (lin_key.astype(jnp.float32) * jnp.exp(last[None, :] - cum.T)[:, :, None]).astype(
        jnp.bfloat16
    )
    local_state = jnp.einsum("thd,the->hde", decayed, lin_value, preferred_element_type=jnp.float32)
    position = lax.axis_index("ctx")
    count = lax.axis_size("ctx")
    totals = lax.all_gather(last, "ctx", axis=0, tiled=True).reshape(count, heads)
    inclusive = jnp.cumsum(totals, axis=0)
    mine = lax.dynamic_index_in_dim(inclusive, position, 0, keepdims=False) - last
    piece = lax.all_gather(local_state[None], "ctx", axis=0, tiled=True)
    length = piece.shape[0]
    index = jnp.arange(length)
    exponent = jnp.where((index < position)[:, None], mine[None, :] - inclusive, -1e30)
    carried = jnp.einsum("mh,mhde->hde", jnp.exp(exponent), piece, precision=lax.Precision.HIGHEST)
    inter = jnp.einsum(
        "thd,hde->the", lin_query, carried.astype(jnp.bfloat16), preferred_element_type=jnp.float32
    )
    raw = intra + inter * jnp.exp(cum).T[:, :, None]
    normed = raw * lax.rsqrt(jnp.mean(raw * raw, axis=-1, keepdims=True) + 1e-06)
    return normed.astype(jnp.bfloat16)


def tile_update(query, query_pos, keys, values, key_start, scale, state):
    running, total, summed = state
    block = keys.shape[0]
    scores = jnp.einsum("thd,shd->hts", query, keys, preferred_element_type=jnp.float32) * scale
    allowed = (query_pos[:, None] >= key_start + jnp.arange(block)[None, :])[None]
    scores = jnp.where(allowed, scores, -1e30)
    updated = jnp.maximum(running, jnp.max(scores, axis=-1))
    probs = jnp.where(allowed, jnp.exp(scores - updated[:, :, None]), 0.0)
    correction = jnp.exp(running - updated)
    total = total * correction + jnp.sum(probs, axis=-1)
    decay_product = jnp.einsum(
        "hts,she->the", probs.astype(jnp.bfloat16), values, preferred_element_type=jnp.float32
    )
    summed = summed * correction.T[:, :, None] + decay_product
    return (updated, total, summed)


def fresh_state(heads, count, width):
    return (
        jnp.full((heads, count), -1e30, jnp.float32),
        jnp.zeros((heads, count), jnp.float32),
        jnp.zeros((count, heads, width), jnp.float32),
    )


def softmax_block(soft_query, soft_key, soft_value):
    rows = soft_query.shape[0]
    heads = soft_query.shape[1]
    width = soft_query.shape[2]
    scale = 1.0 / math.sqrt(width)
    position = lax.axis_index("ctx")
    first_row = position * rows
    query_pos = first_row + jnp.arange(rows)
    start_state = fresh_state(heads, rows, width)
    key_piece = lax.all_gather(soft_key, "ctx", axis=0, tiled=True)
    value_piece = lax.all_gather(soft_value, "ctx", axis=0, tiled=True)
    length = key_piece.shape[0]
    block = math.gcd(512, length)

    def one_tile(step, state):
        keys = lax.dynamic_slice_in_dim(key_piece, step * block, block, 0)
        values = lax.dynamic_slice_in_dim(value_piece, step * block, block, 0)
        key_start = step * block
        return tile_update(soft_query, query_pos, keys, values, key_start, scale, state)

    combined_summary = lax.fori_loop(0, length // block, one_tile, start_state)
    running, total, summed = combined_summary
    return (summed / total.T[:, :, None]).astype(jnp.bfloat16)


def on_device(lin_query, lin_key, lin_value, log_decay, soft_query, soft_key, soft_value):
    linear_out = lightning_block(lin_query, lin_key, lin_value, log_decay)
    softmax_out = softmax_block(soft_query, soft_key, soft_value)
    return (linear_out, softmax_out)


def solution(mesh):
    return jax.shard_map(
        on_device,
        mesh=mesh,
        in_specs=(
            P("ctx", "tp", None),
            P("ctx", "tp", None),
            P("ctx", "tp", None),
            P("tp", "ctx"),
            P("ctx", "tp", None),
            P("ctx", "tp", None),
            P("ctx", "tp", None),
        ),
        out_specs=(P("ctx", "tp", None), P("ctx", "tp", None)),
        check_vma=False,
    )
```

profile of v0, /device:TPU:0, one launch (start us, length us, event | category | flops | bytes accessed | tf_op | source)
XLA Modules:
  0.0 46.2 jit_solution(3535993544773209766)
XLA Ops:
  0.6 0.0 copy-start
  0.7 0.0 copy-start.7
  0.7 0.7 %copy-done.7 = u32[32]{0:T(128)S(1)} copy-done((u32[32]{0:T(128)S(1)}, u32[32]{0:T(128)}, u32[]{:S(2)}) %copy-start.7) | copy-done | bytes 152
  1.3 0.6 %dynamic-slice = u32[1]{0:T(128)} dynamic-slice(u32[32]{0:T(128)S(1)} %copy-done.7, u32[]{:T(128)S(6)} %add.86), dynamic_slice_sizes={1} | dynamic-slice | bytes 12
  2.0 0.0 copy-start.5
  2.0 0.7 %copy-done.5 = f32[1,512]{1,0:T(1,128)S(1)} copy-done((f32[1,512]{1,0:T(1,128)S(1)}, f32[1,512]{1,0:T(1,128)}, u32[]{:S(2)}) %copy-start.5) | copy-done | bytes 2072
  2.6 0.3 reduce-window.6
  2.9 0.6 %slice.12 = f32[1,1]{1,0:T(1,128)} slice(f32[1,512]{1,0:T(1,128)S(1)} %bitcast.108), slice={[0:1], [511:512]} | slice | bytes 8 | tf_op jit(solution)/shard_map/slice | solution.py:19
  3.5 0.2 slice_reduce_fusion
  3.7 0.2 reduce-window.9
  3.9 0.1 broadcast.120
  4.0 0.6 %slice.13 = f32[1,1]{1,0:T(1,128)} slice(f32[1,512]{1,0:T(1,128)S(1)} %bitcast.109), slice={[0:1], [511:512]} | slice | bytes 8 | tf_op jit(solution)/shard_map/slice | solution.py:19
  5.9 0.7 %bitcast_dynamic-update-slice_fusion = f32[4]{0:T(128)S(1)} fusion(f32[4]{0:T(128)S(1)} %broadcast.121, u32[]{:T(128)} %bitcast.12, f32[1,1]{1,0:T(1,128)} %reduce_window_sum.53), kind=kLoop, calls=%fused_computation.67 | loop fusion | bytes 24
  6.5 8.3 %all-reduce = f32[4]{0:T(128)S(1)} all-reduce(f32[4]{0:T(128)S(1)} %bitcast_dynamic-update-slice_fusion), channel_id=2, replica_groups=mesh['ctx'=4,'tp'=8] {'ctx'}, use_global_device_ids=true, to_apply=%add | all-reduce | flops 4 | bytes 32
  14.9 0.1 copy.17
  15.0 0.5 %fusion.52 = f32[1,1]{1,0:T(1,128)} fusion(f32[1,1]{1,0:T(1,128)} %reduce_window_sum.53, f32[4,1]{1,0:T(4,128)S(1)} %reduce_window_sum.54, s32[]{:T(128)S(6)} %select_n.54), kind=kLoop, calls=%fused_computation.72 | loop fusion | flops 1 | bytes 16 | tf_op jit(solution)/shard_map/sub | solution.py:28
  15.5 0.8 %exponential_reduce_fusion = f32[4]{0:T(128)S(1)} fusion(f32[4,1]{1,0:T(4,128)S(1)} %reduce_window_sum.54, f32[]{:T(128)} %bitcast.14, s32[]{:T(128)S(6)} %axis_index.19), kind=kLoop, calls=%fused_computation.63 | loop fusion | flops 12 | bytes 40 | tf_op jit(solution)/shard_map/exp | solution.py:33
  16.3 0.1 subtract_exponential_fusion.1
  16.4 1.3 %fusion.37 = f32[128,128]{1,0:T(8,128)S(1)} fusion(bf16[512,1,128]{2,0,1:T(8,128)(2,1)} %param.10, bf16[512,1,128]{2,0,1:T(8,128)(2,1)} %param.11, f32[512]{0:T(512)S(1)} %get-tuple-element.198), kind=kOutput, calls=%fused_computation.51 | convolution fusion | flops 16973824 | bytes 329728 | tf_op jit(solution)/shard_map/thd,the->hde/dot_general | solution.py:23
  17.7 5.8 %all-gather.1 = f32[512,128]{1,0:T(8,128)S(1)} all-gather(f32[128,128]{1,0:T(8,128)S(1)} %fusion.37), channel_id=3, replica_groups=mesh['ctx'=4,'tp'=8] {'ctx'}, dimensions={0}, use_global_device_ids=true | all-gather | bytes 327680 | tf_op jit(solution)/shard_map/all_gather | solution.py:29
  23.5 0.7 %fusion.34 = f32[1,128,128]{2,0,1:T(1,128)S(1)} fusion(f32[4,128,128]{2,1,0:T(8,128)S(1)} %bitcast.102, f32[4]{0:T(128)S(1)} %exponential_reduce_fusion), kind=kOutput, calls=%fused_computation.44 | convolution fusion | flops 786432 | bytes 327696 | tf_op jit(solution)/shard_map/mh,mhde->hde/dot_general | solution.py:33
  24.2 0.0 copy-done
  24.2 0.2 copy-done.3
  24.4 0.1 copy-done.4
  24.4 0.5 %fusion.25 = f32[1,128,512]{2,1,0:T(8,128)S(1)} fusion(f32[512]{0:T(512)S(1)} %get-tuple-element.199, bf16[512,1,128]{2,0,1:T(8,128)(2,1)S(1)} %copy-done.3, bf16[512,1,128]{2,0,1:T(8,128)(2,1)S(1)} %copy-done.4, bf16[512,1,128]{2,0,1:T(8,128)(2,1)S(1)} %copy-done), kind=kOutput, calls=%fused_computation.34 | convolution fusion | flops 135528448 | bytes 657408 | tf_op jit(solution)/shard_map/hts,she->the/dot_general | solution.py:18
  25.0 0.2 multiply_reduce_fusion
  25.2 0.0 copy-start.1
  25.3 0.8 %copy.19 = bf16[512,1,128]{2,0,1:T(8,128)(2,1)} copy(bf16[512,1,128]{0,2,1:T(8,128)(2,1)S(1)} %fusion.39) | data formatting | bytes 262144
  26.0 0.1 copy-done.1
  26.2 7.4 %all_gather.14 = bf16[2048,1,128]{2,0,1:T(8,128)(2,1)S(1)} all-gather(bf16[512,1,128]{2,0,1:T(8,128)(2,1)S(1)} %copy-done.1), channel_id=1, replica_groups=mesh['ctx'=4,'tp'=8] {'ctx'}, dimensions={0}, use_global_device_ids=true | all-gather | bytes 655360 | tf_op jit(solution)/shard_map/all_gather | solution.py:76
  33.6 0.0 copy-done.2
  33.6 7.4 %all_gather.15 = bf16[2048,1,128]{2,0,1:T(8,128)(2,1)S(1)} all-gather(bf16[512,1,128]{2,0,1:T(8,128)(2,1)S(1)} %copy-done.2), channel_id=1, replica_groups=mesh['ctx'=4,'tp'=8] {'ctx'}, dimensions={0}, use_global_device_ids=true | all-gather | bytes 655360 | tf_op jit(solution)/shard_map/all_gather | solution.py:77
  41.0 0.0 copy-done.6
  41.0 4.2 %while.18 = (s32[]{:T(128)}, f32[1,512]{1,0:T(1,128)S(1)}, f32[1,512]{1,0:T(1,128)S(1)}, f32[512,1,128]{0,2,1:T(8,128)S(1)}, bf16[2048,1,128]{2,0,1:T(8,128)(2,1...) while((s32[]{:T(128)}, f32[1,512]{1,0:T(1,128)S(1)}, ...), condition=%wide.region_7.8_spmd.clone, body=%wide.region_4.7_spmd.clone.sunk | while | flops 137563648 | bytes 4112583 | solution.py:87
  41.0 0.3 fusion.62
  41.3 0.2 fusion.64
  41.6 0.4 fusion.66
  42.0 0.3 fusion.62
  42.4 0.2 fusion.64
  42.6 0.4 fusion.66
  43.1 0.3 fusion.62
  43.5 0.2 fusion.64
  43.7 0.4 fusion.66
  44.2 0.3 fusion.62
  44.5 0.2 fusion.64
  44.8 0.4 fusion.66
  45.2 0.1 copy.18
  45.4 0.8 %divide_convert_fusion = bf16[512,1,128]{2,0,1:T(8,128)(2,1)} fusion(f32[512,1,128]{2,0,1:T(8,128)S(1)} %copy.18, f32[512]{0:T(512)S(1)} %bitcast.106), kind=kLoop, calls=%fused_computation.46 | loop fusion | flops 131072 | bytes 395264 | tf_op jit(solution)/shard_map/convert_element_type | solution.py:89
  (29 shorter events, 0.2 us)
Async XLA Ops:
  0.6 23.5 %copy-start = (bf16[512,1,128]{2,0,1:T(8,128)(2,1)S(1)}, bf16[512,1,128]{2,0,1:T(8,128)(2,1)}, u32[]{:S(2)}) copy-start(bf16[512,1,128]{2,0,1:T(8,128)(2,1)} %param.9) | copy-start | bytes 393220
  0.7 0.7 %copy-start.7 = (u32[32]{0:T(128)S(1)}, u32[32]{0:T(128)}, u32[]{:S(2)}) copy-start(u32[32]{0:T(128)} %constant.93) | copy-start | bytes 388
  2.0 0.7 %copy-start.5 = (f32[1,512]{1,0:T(1,128)S(1)}, f32[1,512]{1,0:T(1,128)}, u32[]{:S(2)}) copy-start(f32[1,512]{1,0:T(1,128)} %param.12) | copy-start | bytes 6148
  23.5 0.9 %copy-start.3 = (bf16[512,1,128]{2,0,1:T(8,128)(2,1)S(1)}, bf16[512,1,128]{2,0,1:T(8,128)(2,1)}, u32[]{:S(2)}) copy-start(bf16[512,1,128]{2,0,1:T(8,128)(2,1)} %param.11) | copy-start | bytes 393220
  23.5 1.0 %copy-start.4 = (bf16[512,1,128]{2,0,1:T(8,128)(2,1)S(1)}, bf16[512,1,128]{2,0,1:T(8,128)(2,1)}, u32[]{:S(2)}) copy-start(bf16[512,1,128]{2,0,1:T(8,128)(2,1)} %param.10) | copy-start | bytes 393220
  25.2 0.9 %copy-start.1 = (bf16[512,1,128]{2,0,1:T(8,128)(2,1)S(1)}, bf16[512,1,128]{2,0,1:T(8,128)(2,1)}, u32[]{:S(2)}) copy-start(bf16[512,1,128]{2,0,1:T(8,128)(2,1)} %param.14) | copy-start | bytes 393220
  26.2 7.4 %copy-start.2 = (bf16[512,1,128]{2,0,1:T(8,128)(2,1)S(1)}, bf16[512,1,128]{2,0,1:T(8,128)(2,1)}, u32[]{:S(2)}) copy-start(bf16[512,1,128]{2,0,1:T(8,128)(2,1)} %param.15) | copy-start | bytes 393220
  33.6 7.4 %copy-start.6 = (bf16[512,1,128]{2,0,1:T(8,128)(2,1)S(1)}, bf16[512,1,128]{2,0,1:T(8,128)(2,1)}, u32[]{:S(2)}) copy-start(bf16[512,1,128]{2,0,1:T(8,128)(2,1)} %param.13) | copy-start | bytes 393220
where the time goes:
time: 46.5 us; the launch traced here: 46.2 us
  blocking collectives  28.9 us (62%)
  matrix products  5.65 us (12%)
  local copies, waits for them, and re-layouts  5.48 us (12%)
  other arithmetic  3.81 us (8%)
  between operations  2.06 us (4%)
    unnamed x1, blocking collectives  8.34 us
    all_gather x1, blocking collectives, softmax_block(): value_piece = lax.all_gather(soft_value, 'ctx', axis=0, tiled=True)  7.41 us
    all_gather x1, blocking collectives, softmax_block(): key_piece = lax.all_gather(soft_key, 'ctx', axis=0, tiled=True)  7.41 us
    all_gather x1, blocking collectives, lightning_block(): piece = lax.all_gather(local_state[None], 'ctx', axis=0, tiled=True)  5.79 us
    unnamed x21, local copies, waits for them, and re-layouts  3.92 us
    dot_general x4, matrix products, tile_update(): jnp.einsum('hts,she->the', probs.astype(jnp.bfloat16), values, preferred_...  1.64 us
    dot_general x1, matrix products, lightning_block(): jnp.einsum('thd,the->hde', decayed, lin_value, preferred_element_type=jnp...  1.3 us
    dot_general x4, matrix products, tile_update(): jnp.einsum('thd,shd->hts', query, keys, preferred_element_type=jnp.float32)  1.29 us

commit v1 on v0

v1 whole, which is shorter than its diff:
```python
import functools
import math

import jax
import jax.numpy as jnp
from jax import lax
from jax.experimental import pallas as pl
from jax.experimental.pallas import tpu as pltpu
from jax.sharding import PartitionSpec as P

NEG = -1e30
TINY = 1e-6
PAD = 16
F32 = jnp.float32
BF16 = jnp.bfloat16
VMEM = pltpu.VMEM


def dot(a, b, contract):
    return lax.dot_general(a, b, (contract, ((), ())), preferred_element_type=F32)


def dot_nn(a, b):
    return dot(a, b, ((1,), (0,)))


def dot_nt(a, b):
    return dot(a, b, ((1,), (1,)))


def dot_tn(a, b):
    return dot(a, b, ((0,), (0,)))


def three_parts(x):
    high = x.astype(BF16)
    rest = x - high.astype(F32)
    middle = rest.astype(BF16)
    low = (rest - middle.astype(F32)).astype(BF16)
    return high, middle, low


def iota(shape, dim):
    return lax.broadcasted_iota(jnp.int32, shape, dim)


def select_rows(parts, rows, width):
    row = iota((rows, width), 0)
    out = jnp.zeros((rows, width), F32)
    for number, part in enumerate(parts):
        out = jnp.where(row == number, part.astype(F32), out)
    return out.astype(BF16)


def state_kernel(decay_ref, key_ref, value_ref, soft_value_ref, pack_ref, cum_row_ref, cum_col_ref):
    rows, width = key_ref.shape
    parts = select_rows(three_parts(decay_ref[...]), PAD, rows)
    upto = (iota((rows, rows), 0) <= iota((rows, rows), 1)).astype(F32).astype(BF16)
    cum_row = jnp.sum(dot_nn(parts, upto), axis=0, keepdims=True)
    cum_row_ref[...] = cum_row
    cum_col = jnp.transpose(jnp.broadcast_to(cum_row, (width, rows)))
    cum_col_ref[...] = cum_col
    total = cum_col[rows - 1 :, :]
    decayed = (key_ref[...].astype(F32) * jnp.exp(total - cum_col)).astype(BF16)
    state = dot_tn(decayed, value_ref[...])
    high = state.astype(BF16)
    pack_ref[:rows, :] = soft_value_ref[...]
    pack_ref[rows : rows + width, :] = high
    pack_ref[rows + width : rows + 2 * width, :] = (state - high.astype(F32)).astype(BF16)
    pack_ref[rows + 2 * width :, :] = select_rows(three_parts(total), PAD, width)


def local_kernel(
    scale, step,
    lin_q_ref, lin_k_ref, lin_v_ref, cum_row_ref, cum_col_ref, q_ref, k_ref, v_ref,
    intra_ref, top_ref, total_ref, summed_ref,
):
    rows, width = lin_q_ref.shape
    lower = iota((step, step), 0) >= iota((step, step), 1)
    for start in range(0, rows, step):
        stop = start + step
        mine = pl.ds(start, step)
        scores = dot_nt(lin_q_ref[mine, :], lin_k_ref[:stop, :])
        cum_t = cum_col_ref[mine, :1]
        weights = []
        for left in range(0, stop, step):
            diff = cum_t - cum_row_ref[:, left : left + step]
            if left == start:
                diff = jnp.where(lower, diff, NEG)
            weights.append((scores[:, left : left + step] * jnp.exp(diff)).astype(BF16))
        weights = jnp.concatenate(weights, axis=1) if len(weights) > 1 else weights[0]
        intra_ref[mine, :] = dot_nn(weights, lin_v_ref[:stop, :])

        scores = dot_nt(q_ref[mine, :], k_ref[:stop, :])
        last = jnp.where(lower, scores[:, start:], NEG)
        scores = jnp.concatenate([scores[:, :start], last], axis=1) if start else last
        top = jnp.max(scores, axis=1, keepdims=True)
        probs = jnp.exp2((scores - top) * scale)
        total = jnp.sum(probs, axis=1, keepdims=True)
        top_ref[mine, :] = jnp.broadcast_to(top, (step, width))
        total_ref[mine, :] = jnp.broadcast_to(total, (step, width))
        summed_ref[mine, :] = dot_nn(probs.astype(BF16), v_ref[:stop, :])


def block_numbers(axis, cores, chips):
    position = lax.axis_index(axis)
    if cores == 1:
        return position, [position - apart for apart in range(1, chips)]
    other = lax.rem(position, 2)
    partner = position + 1 - 2 * other
    numbers = [jnp.where(other == 1, position - 1, -1)]
    for apart in range(1, chips):
        numbers += [position - 2 * apart, partner - 2 * apart]
    return position, numbers


def score_kernel(scale, step, axis, cores, chips, q_ref, top_ref, total_ref, *refs):
    key_refs, (probs_ref, factor_ref, sum_ref) = refs[:-3], refs[-3:]
    rows, width = q_ref.shape
    _, numbers = block_numbers(axis, cores, chips)
    away = [jnp.where(number >= 0, 0.0, NEG) for number in numbers]
    for start in range(0, rows, step):
        mine = pl.ds(start, step)
        query = q_ref[mine, :]
        old = top_ref[mine, :1]
        scores = [dot_nt(query, key_ref[...]) for key_ref in key_refs]
        top = old
        for score, off in zip(scores, away):
            top = jnp.maximum(top, jnp.max(score, axis=1, keepdims=True) + off)
        factor = jnp.exp2((old - top) * scale)
        total = total_ref[mine, :1] * factor
        for number, (score, off) in enumerate(zip(scores, away)):
            probs = jnp.exp2((score - (top - off)) * scale)
            total = total + jnp.sum(probs, axis=1, keepdims=True)
            probs_ref[mine, number * rows : (number + 1) * rows] = probs.astype(BF16)
        factor_ref[mine, :] = jnp.broadcast_to(factor, (step, width))
        sum_ref[mine, :] = jnp.broadcast_to(total, (step, width))


def finish_kernel(
    step, axis, cores, chips,
    lin_q_ref, intra_ref, cum_col_ref, summed_ref, probs_ref, factor_ref, sum_ref, *refs,
):
    pack_refs, (linear_ref, softmax_ref) = refs[:-2], refs[-2:]
    rows, width = lin_q_ref.shape
    position, numbers = block_numbers(axis, cores, chips)
    totals, states = [], []
    for pack_ref in pack_refs:
        tail = pack_ref[rows + 2 * width :, :].astype(F32)
        totals.append(tail[0:1] + tail[1:2] + tail[2:3])
        states.append(
            pack_ref[rows : rows + width, :].astype(F32)
            + pack_ref[rows + width : rows + 2 * width, :].astype(F32)
        )
    carried = jnp.zeros((width, width), F32)
    for number, state in zip(numbers, states):
        between = jnp.where(number >= 0, 0.0, NEG)
        for other, total in zip(numbers, totals):
            between = between + jnp.where(other > number, 1.0, 0.0) * total
        carried = carried + jnp.exp(between) * state
    carried = carried.astype(BF16)
    for start in range(0, rows, step):
        mine = pl.ds(start, step)
        summed = summed_ref[mine, :] * factor_ref[mine, :]
        for number, pack_ref in enumerate(pack_refs):
            summed = summed + dot_nn(
                probs_ref[mine, number * rows : (number + 1) * rows], pack_ref[:rows, :]
            )
        softmax_ref[mine, :] = (summed / sum_ref[mine, :]).astype(BF16)
        inter = dot_nn(lin_q_ref[mine, :], carried)
        raw = intra_ref[mine, :] + inter * jnp.exp(cum_col_ref[mine, :])
        square = jnp.sum(raw * raw, axis=1, keepdims=True) * (1.0 / width)
        linear_ref[mine, :] = (raw * lax.rsqrt(square + TINY)).astype(BF16)


def call(body, operands, outs, flops):
    size = sum(math.prod(x.shape) * x.dtype.itemsize for x in (*operands, *outs))
    return pl.pallas_call(
        body,
        out_shape=tuple(outs),
        in_specs=[pl.BlockSpec(memory_space=VMEM)] * len(operands),
        out_specs=tuple(pl.BlockSpec(memory_space=VMEM) for _ in outs),
        cost_estimate=pl.CostEstimate(flops=flops, bytes_accessed=size, transcendentals=0),
    )(*operands)


def on_device(axis, lin_query, lin_key, lin_value, log_decay, soft_query, soft_key, soft_value):
    rows, heads, width = lin_query.shape
    count = lax.axis_size(axis)
    cores = 2 if count % 2 == 0 else 1
    chips = count // cores

    def to_partner(x):
        return lax.ppermute(x, axis, [(2 * chip, 2 * chip + 1) for chip in range(chips)])

    def across(x, apart):
        apart = apart * cores
        return lax.ppermute(x, axis, [(i, i + apart) for i in range(count - apart)])

    def swapped(x):
        return lax.ppermute(x, axis, [(i, i ^ 1) for i in range(count)])

    def spread(x):
        own = [to_partner(x)] if cores == 2 else []
        far = [across(x, apart) for apart in range(1, chips)]
        out = list(own)
        for block in far:
            out.append(block)
            if cores == 2:
                out.append(swapped(block))
        return out

    def one_head(lq, lk, lv, decay, sq, sk, sv):
        step = math.gcd(rows, 128)
        scale = math.log2(math.e) / math.sqrt(width)
        shape = jax.ShapeDtypeStruct
        flat = shape((rows, width), F32)
        keys = spread(sk)
        pack, cum_row, cum_col = call(
            state_kernel,
            (decay, lk, lv, sv),
            (shape((rows + 2 * width + PAD, width), BF16), shape((1, rows), F32), flat),
            2 * rows * width * width,
        )
        packs = spread(pack)
        intra, top, total, summed = call(
            functools.partial(local_kernel, scale, step),
            (lq, lk, lv, cum_row, cum_col, sq, sk, sv),
            (flat, flat, flat, flat),
            8 * rows * rows * width,
        )
        blocks = len(keys)
        ring = (axis, cores, chips)
        probs, factor, sums = call(
            functools.partial(score_kernel, scale, step, *ring),
            (sq, top, total, *keys),
            (shape((rows, blocks * rows), BF16), flat, flat),
            2 * blocks * rows * rows * width,
        )
        out = shape((rows, width), BF16)
        return call(
            functools.partial(finish_kernel, step, *ring),
            (lq, intra, cum_col, summed, probs, factor, sums, *packs),
            (out, out),
            2 * blocks * rows * rows * width,
        )

    outs = [
        one_head(
            *(x[:, head] for x in (lin_query, lin_key, lin_value)),
            log_decay[head : head + 1],
            *(x[:, head] for x in (soft_query, soft_key, soft_value)),
        )
        for head in range(heads)
    ]
    linear = jnp.stack([pair[0] for pair in outs], axis=1)
    softmax = jnp.stack([pair[1] for pair in outs], axis=1)
    return linear, softmax


def solution(mesh):
    block = P("ctx", "tp", None)
    return jax.shard_map(
        functools.partial(on_device, "ctx"),
        mesh=mesh,
        in_specs=(block, block, block, P("tp", "ctx"), block, block, block),
        out_specs=(block, block),
        check_vma=False,
    )
```

time: 46.5 us -> 29.8 us (0.64)
  blocking collectives: 28.9 us -> 0 us
  Pallas kernels: 0 us -> 14.3 us
  starting transfers between devices: 0 us -> 10.1 us
  matrix products: 5.65 us -> 0 us
  local copies, waits for them, and re-layouts: 5.48 us -> 1.4 us
  other arithmetic: 3.81 us -> 0 us
  waiting for transfers between devices: 0 us -> 2.91 us
  between operations: 2.06 us -> 0.74 us
    all_gather x3 -> x0, blocking collectives: 20.6 us -> none  [the longest x1 7.41 us: softmax_block(): value_piece = lax.all_gather(soft_value, 'ctx', axis=0, tiled=True)]
    pallas_call x0 -> x4, Pallas kernels: none -> 14.3 us  [call(): pl.pallas_call(body, out_shape=tuple(outs), in_specs=[pl.BlockSpec(memory...]
    ppermute x0 -> x6, starting transfers between devices: none -> 10.1 us  [the longest x2 6.14 us: across(): return lax.ppermute(x, axis, [(i, i + apart) for i in range(count - apart)])]
    unnamed x1 -> x0, blocking collectives: 8.34 us -> none
    dot_general x12 -> x0, matrix products: 5.65 us -> none  [the longest x4 1.64 us: tile_update(): jnp.einsum('hts,she->the', probs.astype(jnp.bfloat16), values, preferred_...]
    ppermute x0 -> x6, waiting for transfers between devices: none -> 2.91 us  [the longest x2 2.9 us: across(): return lax.ppermute(x, axis, [(i, i + apart) for i in range(count - apart)])]
    unnamed x21 -> x12, local copies, waits for them, and re-layouts: 3.92 us -> 1.4 us
    slice x3 -> x0, local copies, waits for them, and re-layouts: 1.35 us -> none  [the longest x2 1.17 us: lightning_block(): last = cum[:, -1]]
  transfers between devices with their start and end apart: 0 -> 6, of which waited for: 0 -> 1; matrix products, arithmetic and copies ran while one was open for 0% -> 0% of each run, Pallas kernels for 0% -> 30%
where the time goes in v1:
time: 29.8 us; the launch traced here: 29.4 us
  Pallas kernels  14.3 us (48%)
  starting transfers between devices  10.1 us (34%)
  waiting for transfers between devices  2.91 us (10%)
  local copies, waits for them, and re-layouts  1.4 us (5%)
  between operations  0.74 us (2%)
    pallas_call x4, Pallas kernels, call(): pl.pallas_call(body, out_shape=tuple(outs), in_specs=[pl.BlockSpec(memory...  14.3 us
    ppermute x2, starting transfers between devices, across(): return lax.ppermute(x, axis, [(i, i + apart) for i in range(count - apart)])  6.14 us
    ppermute x2, starting transfers between devices, to_partner(): lax.ppermute(x, axis, [(2 * chip, 2 * chip + 1) for chip in range(chips)])  3.88 us
    ppermute x2, waiting for transfers between devices, across(): return lax.ppermute(x, axis, [(i, i + apart) for i in range(count - apart)])  2.9 us
    unnamed x12, local copies, waits for them, and re-layouts  1.4 us
  transfers between devices with their start and end apart: 6, of which 1 were waited for; matrix products, arithmetic and copies ran while one was open for 0% of the time, Pallas kernels for 30%

profile of v1, /device:TPU:0, one launch (start us, length us, event | category | flops | bytes accessed | tf_op | source)
XLA Modules:
  0.0 29.4 jit_solution(7324089913084476756)
XLA Ops:
  0.6 2.3 %shard_map.86 = (bf16[784,128]{1,0:T(8,128)(2,1)}, f32[1,512]{1,0:T(1,128)}, f32[512,128]{1,0:T(8,128)}) custom-call(f32[1,512]{1,0:T(1,128)} %decay_ref.1, bf16[512,128]{1,0:T(8,128)(2,1)} %bitcast.8, bf16[512,128]{1,0:T(8,128)(2,1)} %bitcast.10, bf16[512,128]{1,0:T(8,128)(2,1)} %bitcast.12), custom_call_target="tpu_custom_call" | custom-call | flops 16777216 | bytes 860160 | tf_op jit(solution)/shard_map/pallas_call | solution.py:178
  2.9 4.8 %collective-permute-start.4 = (bf16[784,128]{1,0:T(8,128)(2,1)}, bf16[784,128]{1,0:T(8,128)(2,1)S(1)}, u32[]{:S(2)}, u32[]{:S(2)}) collective-permute-start(bf16[784,128]{1,0:T(8,128)(2,1)} %get-tuple-element.23), channel_id=1, source_target_pairs={{0,16},{8,24},{1,17},{9,25},{2,18},{10,26},{3,19},{11,27},{4,20},{... | collective-permute-start | bytes 602120 | tf_op jit(solution)/shard_map/ppermute | solution.py:198
  7.8 1.3 %collective-permute-start.1 = (bf16[512,128]{1,0:T(8,128)(2,1)}, bf16[512,128]{1,0:T(8,128)(2,1)S(1)}, u32[]{:S(2)}, u32[]{:S(2)}) collective-permute-start(bf16[512,128]{1,0:T(8,128)(2,1)} %bitcast.18), channel_id=1, source_target_pairs={{0,16},{8,24},{1,17},{9,25},{2,18},{10,26},{3,19},{11,27},{4,20},{... | collective-permute-start | bytes 393224 | tf_op jit(solution)/shard_map/ppermute | solution.py:198
  9.1 1.5 %collective-permute-start.3 = (bf16[784,128]{1,0:T(8,128)(2,1)}, bf16[784,128]{1,0:T(8,128)(2,1)S(1)}, u32[]{:S(2)}, u32[]{:S(2)}) collective-permute-start(bf16[784,128]{1,0:T(8,128)(2,1)} %get-tuple-element.23), channel_id=1, source_target_pairs={{0,8},{16,24},{1,9},{17,25},{2,10},{18,26},{3,11},{19,27},{4,12},{... | collective-permute-start | bytes 602120 | tf_op jit(solution)/shard_map/ppermute | solution.py:194
  10.5 2.9 %collective-permute-done.4.refs_1_ = bf16[784,128]{1,0:T(8,128)(2,1)S(1)} collective-permute-done((bf16[784,128]{1,0:T(8,128)(2,1)}, bf16[784,128]{1,0:T(8,128)(2,1)S(1)}, u32[]{:S(2)}, u32[]{:S(2)}) %collective-permute-start.4) | collective-permute-done | bytes 200736 | tf_op jit(solution)/shard_map/ppermute | solution.py:198
  13.4 0.0 copy-start
  13.4 0.0 collective-permute-start.5
  13.4 2.4 %collective-permute-start = (bf16[512,128]{1,0:T(8,128)(2,1)}, bf16[512,128]{1,0:T(8,128)(2,1)S(1)}, u32[]{:S(2)}, u32[]{:S(2)}) collective-permute-start(bf16[512,128]{1,0:T(8,128)(2,1)} %bitcast.19), channel_id=1, source_target_pairs={{0,8},{16,24},{1,9},{17,25},{2,10},{18,26},{3,11},{19,27},{4,12},{... | collective-permute-start | bytes 393224 | tf_op jit(solution)/shard_map/ppermute | solution.py:194
  15.9 0.0 collective-permute-done.1.refs_1_
  15.9 0.0 copy-start.3
  15.9 0.1 collective-permute-start.2
  16.0 3.8 %shard_map.87 = (f32[512,128]{1,0:T(8,128)}, f32[512,128]{1,0:T(8,128)}, f32[512,128]{1,0:T(8,128)}, f32[512,128]{1,0:T(8,128)}) custom-call(bf16[512,128]{1,0:T(8,128)(2,1)} %bitcast.14, bf16[512,128]{1,0:T(8,128)(2,1)} %bitcast.9, bf16[512,128]{1,0:T(8,128)(2,1)} %bitcast.11, f32[1,512]{1,0:T(1,128)} %get-tuple-element.14.cum_row_ref, ...), custom_call_target="tpu_custom_call" | custom-call | flops 268435456 | bytes 2099200 | tf_op jit(solution)/shard_map/pallas_call | solution.py:178
  19.8 0.0 collective-permute-done.refs_0_
  19.8 0.0 copy-start.4
  19.8 0.0 collective-permute-done.2.refs_2_
  19.8 0.0 copy-start.5
  19.8 0.0 copy-done.3
  19.8 0.6 %copy-done.4 = bf16[512,128]{1,0:T(8,128)(2,1)} copy-done((bf16[512,128]{1,0:T(8,128)(2,1)}, bf16[512,128]{1,0:T(8,128)(2,1)S(1)}, u32[]{:S(2)}) %copy-start.4) | copy-done | bytes 131096
  20.5 0.0 copy-done.5
  20.5 4.9 %shard_map.88 = (bf16[512,1536]{1,0:T(8,128)(2,1)}, f32[512,128]{1,0:T(8,128)}, f32[512,128]{1,0:T(8,128)}) custom-call(bf16[512,128]{1,0:T(8,128)(2,1)} %bitcast.17, f32[512,128]{1,0:T(8,128)} %get-tuple-element.18.top_ref, f32[512,128]{1,0:T(8,128)} %get-tuple-element.19.total_ref, bf16[512,128]{1,0:T(8,128)(2,1)} %copy-done.4, ...), custom_call_target="tpu_custom_call" | custom-call | flops 201326592 | bytes 3145728 | tf_op jit(solution)/shard_map/pallas_call | solution.py:178
  25.4 0.0 collective-permute-done.3.refs_0_
  25.4 0.0 copy-start.1
  25.4 0.0 collective-permute-done.5.refs_2_
  25.4 0.0 copy-start.2
  25.4 0.0 copy-done
  25.4 0.7 %copy-done.1 = bf16[784,128]{1,0:T(8,128)(2,1)} copy-done((bf16[784,128]{1,0:T(8,128)(2,1)}, bf16[784,128]{1,0:T(8,128)(2,1)S(1)}, u32[]{:S(2)}) %copy-start.1) | copy-done | bytes 200728
  26.1 0.1 copy-done.2
  26.1 3.3 %shard_map.89 = (bf16[512,128]{1,0:T(8,128)(2,1)}, bf16[512,128]{1,0:T(8,128)(2,1)}) custom-call(bf16[512,128]{1,0:T(8,128)(2,1)} %bitcast.15, f32[512,128]{1,0:T(8,128)} %get-tuple-element.16.intra_ref, f32[512,128]{1,0:T(8,128)} %get-tuple-element.15.cum_col_ref, f32[512,128]{1,0:T(8,128)} %get-tuple-element.17.summed_ref, ...), custom_call_target="tpu_custom_call" | custom-call | flops 201326592 | bytes 3878912 | tf_op jit(solution)/shard_map/pallas_call | solution.py:178
Async XLA Ops:
  2.9 10.5 %collective-permute-start.4 = (bf16[784,128]{1,0:T(8,128)(2,1)}, bf16[784,128]{1,0:T(8,128)(2,1)S(1)}, u32[]{:S(2)}, u32[]{:S(2)}) collective-permute-start(bf16[784,128]{1,0:T(8,128)(2,1)} %get-tuple-element.23), channel_id=1, source_target_pairs={{0,16},{8,24},{1,17},{9,25},{2,18},{10,26},{3,19},{11,27},{4,20},{... | collective-permute-start | bytes 602120 | tf_op jit(solution)/shard_map/ppermute | solution.py:198
  7.8 8.1 %collective-permute-start.1 = (bf16[512,128]{1,0:T(8,128)(2,1)}, bf16[512,128]{1,0:T(8,128)(2,1)S(1)}, u32[]{:S(2)}, u32[]{:S(2)}) collective-permute-start(bf16[512,128]{1,0:T(8,128)(2,1)} %bitcast.18), channel_id=1, source_target_pairs={{0,16},{8,24},{1,17},{9,25},{2,18},{10,26},{3,19},{11,27},{4,20},{... | collective-permute-start | bytes 393224 | tf_op jit(solution)/shard_map/ppermute | solution.py:198
  9.1 16.3 %collective-permute-start.3 = (bf16[784,128]{1,0:T(8,128)(2,1)}, bf16[784,128]{1,0:T(8,128)(2,1)S(1)}, u32[]{:S(2)}, u32[]{:S(2)}) collective-permute-start(bf16[784,128]{1,0:T(8,128)(2,1)} %get-tuple-element.23), channel_id=1, source_target_pairs={{0,8},{16,24},{1,9},{17,25},{2,10},{18,26},{3,11},{19,27},{4,12},{... | collective-permute-start | bytes 602120 | tf_op jit(solution)/shard_map/ppermute | solution.py:194
  13.4 11.9 %copy-start = (bf16[784,128]{1,0:T(8,128)(2,1)}, bf16[784,128]{1,0:T(8,128)(2,1)S(1)}, u32[]{:S(2)}) copy-start(bf16[784,128]{1,0:T(8,128)(2,1)S(1)} %collective-permute-done.4.refs_1_) | copy-start | bytes 602116
  13.4 11.9 %collective-permute-start.5 = (bf16[784,128]{1,0:T(8,128)(2,1)S(1)}, bf16[784,128]{1,0:T(8,128)(2,1)S(1)}, u32[]{:S(2)}, u32[]{:S(2)}) collective-permute-start(bf16[784,128]{1,0:T(8,128)(2,1)S(1)} %collective-permute-done.4.refs_1_), channel_id=1, source_target_pairs={{0,8},{8,0},{16,24},{24,16},{1,9},{9,1},{17,25},{25,17},{2,10},{10... | collective-permute-start | bytes 602120 | tf_op jit(solution)/shard_map/ppermute | solution.py:201
  13.4 6.4 %collective-permute-start = (bf16[512,128]{1,0:T(8,128)(2,1)}, bf16[512,128]{1,0:T(8,128)(2,1)S(1)}, u32[]{:S(2)}, u32[]{:S(2)}) collective-permute-start(bf16[512,128]{1,0:T(8,128)(2,1)} %bitcast.19), channel_id=1, source_target_pairs={{0,8},{16,24},{1,9},{17,25},{2,10},{18,26},{3,11},{19,27},{4,12},{... | collective-permute-start | bytes 393224 | tf_op jit(solution)/shard_map/ppermute | solution.py:194
  15.9 4.0 %copy-start.3 = (bf16[512,128]{1,0:T(8,128)(2,1)}, bf16[512,128]{1,0:T(8,128)(2,1)S(1)}, u32[]{:S(2)}) copy-start(bf16[512,128]{1,0:T(8,128)(2,1)S(1)} %collective-permute-done.1.refs_1_) | copy-start | bytes 393220
  15.9 3.9 %collective-permute-start.2 = (bf16[512,128]{1,0:T(8,128)(2,1)S(1)}, bf16[512,128]{1,0:T(8,128)(2,1)S(1)}, u32[]{:S(2)}, u32[]{:S(2)}) collective-permute-start(bf16[512,128]{1,0:T(8,128)(2,1)S(1)} %collective-permute-done.1.refs_1_), channel_id=1, source_target_pairs={{0,8},{8,0},{16,24},{24,16},{1,9},{9,1},{17,25},{25,17},{2,10},{10... | collective-permute-start | bytes 393224 | tf_op jit(solution)/shard_map/ppermute | solution.py:201
  19.8 0.7 %copy-start.4 = (bf16[512,128]{1,0:T(8,128)(2,1)}, bf16[512,128]{1,0:T(8,128)(2,1)S(1)}, u32[]{:S(2)}) copy-start(bf16[512,128]{1,0:T(8,128)(2,1)S(1)} %collective-permute-done.refs_0_) | copy-start | bytes 393220
  19.8 0.7 %copy-start.5 = (bf16[512,128]{1,0:T(8,128)(2,1)}, bf16[512,128]{1,0:T(8,128)(2,1)S(1)}, u32[]{:S(2)}) copy-start(bf16[512,128]{1,0:T(8,128)(2,1)S(1)} %collective-permute-done.2.refs_2_) | copy-start | bytes 393220
  25.4 0.7 %copy-start.1 = (bf16[784,128]{1,0:T(8,128)(2,1)}, bf16[784,128]{1,0:T(8,128)(2,1)S(1)}, u32[]{:S(2)}) copy-start(bf16[784,128]{1,0:T(8,128)(2,1)S(1)} %collective-permute-done.3.refs_0_) | copy-start | bytes 602116
  25.4 0.8 %copy-start.2 = (bf16[784,128]{1,0:T(8,128)(2,1)}, bf16[784,128]{1,0:T(8,128)(2,1)S(1)}, u32[]{:S(2)}) copy-start(bf16[784,128]{1,0:T(8,128)(2,1)S(1)} %collective-permute-done.5.refs_2_) | copy-start | bytes 602116
